TPU v7x, 32 devices: a whole 2x2x4 slice. The times are simulated.
32 devices in a mesh: group: 2 (over y), inst: 4 (over x, core), brick: 4 (over z).
Axes of the slice: x: 2, y: 2, z: 4, core: 2. Of those that a mesh axis runs over, the one named last changes fastest.
Arguments:
- state: float32 [32, 5, 32, 4096], P(('group', 'inst'), None, 'brick'), parts along dimension 0, may hold values from -1.5 to 4, as said below
- time_step: float32 [64, 4096], P(('group', 'brick')), parts along dimension 0, may hold values from 0.05 to 0.5
- blocks: bfloat16 [8, 320, 320], replicated, may hold values from -0.3125 to 0.3125
- cut_counts: int32 [8], P('group'), parts along dimension 0, may hold values from 1 to 256, 384 in all
- tile_index: int32 [8, 256], P(('group', 'brick')), parts along dimension 0, may hold values from 0 to 511, as said below
- tile_type: int32 [8, 256], P(('group', 'brick')), parts along dimension 0, may hold values from 0 to 7
Outputs:
- residual: float32 [32, 5, 32, 4096], P(('group', 'inst'), None, 'brick'), parts along dimension 0
- new_state: float32 [32, 5, 32, 4096], P(('group', 'inst'), None, 'brick'), parts along dimension 0
There are 2 independent parts, one for each index of `group`. A program takes and returns all parts, laid end to end along the dimension named above; an argument that names none is the same for every part. Nothing has to cross between parts.
Inputs may be any that keep to these rules, and one draw needn't show every extreme that they name: `state`: component 0 (density) lies in 0.5 to 2, components 1 to 3 in -1.5 to 1.5, component 4 in 1.5 to 4. `tile_index`: row b lists 256 different tiles of brick b. `cut_counts`: the entries sum to 384.
All inputs are finite; a program needn't handle non-finite values.
Results may differ from a plain program's by a relative error of at most 0.0013.
Values may be sent and summed in bfloat16 or wider, within the bound.
A program may use at most 64 MiB of HBM per device.

v0:
```python
import jax
import jax.numpy as jnp
from jax import lax
from jax.sharding import PartitionSpec as P

NINST = 16
NVAR = 5
TILE = 64
TSIZE = 320
TILES_DEV = 512


GAMMA_MINUS = 0.4
EPS_FOURTH = 0.03125


def padded(cells, sides, width):
    for axis, dim in sides:
        count = lax.axis_size(axis)
        ends = count - 1
        head = lax.slice_in_dim(cells, 0, width, axis=dim)
        tail = lax.slice_in_dim(cells, cells.shape[dim] - width, cells.shape[dim], axis=dim)
        cells = jnp.concatenate(
            [
                lax.ppermute(tail, axis, [(i, (i + 1) % count) for i in range(ends)]),
                cells,
                lax.ppermute(head, axis, [((i + 1) % count, i) for i in range(ends)]),
            ],
            axis=dim,
        )
    return cells


def spectral_entry(diff, count):
    shifted = jnp.mod(diff, count)
    sign = 1.0 - 2.0 * jnp.mod(diff, 2).astype(jnp.float32)
    safe = jnp.where(shifted == 0, 1, shifted).astype(jnp.float32)
    value = sign / jnp.tan(jnp.pi * safe / count)
    return jnp.where(shifted == 0, 0.0, value)


def euler_flux(state):
    density = state[:, 0]
    density = jnp.where(density == 0.0, 1.0, density)
    mom_one = state[:, 1]
    mom_two = state[:, 2]
    mom_three = state[:, 3]
    energy = state[:, 4]
    speed = mom_one / density
    press = GAMMA_MINUS * (
        energy - 0.5 * (mom_one * mom_one + mom_two * mom_two + mom_three * mom_three) / density
    )
    return jnp.stack(
        [
            mom_one,
            mom_one * speed + press,
            mom_two * speed,
            mom_three * speed,
            (energy + press) * speed,
        ],
        axis=1,
    )


def apply_range(states, kinds_row, blocks, lower, upper):
    rows = states.shape[0]
    row_ids = jnp.arange(rows, dtype=jnp.int32)
    keep = (row_ids >= lower) & (row_ids < upper)
    total = jnp.zeros(states.shape, jnp.float32)
    for kind in range(blocks.shape[0]):
        select = keep & (kinds_row == kind)
        masked = jnp.where(select[:, None, None], states, jnp.zeros_like(states))
        total = total + jnp.einsum(
            "ab,tib->tia", blocks[kind], masked, preferred_element_type=jnp.float32
        )
    return total


def per_device(state, time_step, blocks, cut_counts, tile_index, tile_type):
    inst_here = state.shape[0]
    rows_here = state.shape[2]
    row_cells = state.shape[3]
    qpad = padded(state.astype(jnp.bfloat16), (("brick", 2),), 2).astype(state.dtype)
    fpad = euler_flux(qpad)
    transport = 0.5 * (fpad[:, :, 3:-1] - fpad[:, :, 1:-3])
    smoothing = EPS_FOURTH * (
        qpad[:, :, 4:]
        - 4.0 * qpad[:, :, 3:-1]
        + 6.0 * qpad[:, :, 2:-2]
        - 4.0 * qpad[:, :, 1:-3]
        + qpad[:, :, :-4]
    )
    mine = lax.axis_index("inst") * inst_here + jnp.arange(inst_here, dtype=jnp.int32)
    piece = lax.all_gather(state, "inst", axis=0, tiled=True)
    others = jnp.arange(piece.shape[0], dtype=jnp.int32)
    coef = spectral_entry(mine[:, None] - others[None, :], NINST)
    timewise = jnp.einsum("jk,kcxs->jcxs", coef, piece, precision=lax.Precision.HIGHEST)
    tiles = (
        state.reshape(inst_here, NVAR, TILES_DEV, TILE)
        .transpose(2, 0, 1, 3)
        .reshape(TILES_DEV, inst_here, TSIZE)
    )
    index_row = tile_index[0]
    kinds_row = tile_type[0]
    own_states = tiles[index_row].astype(jnp.bfloat16)
    brick_here = lax.axis_index("brick")
    count_here = cut_counts[brick_here]
    results = apply_range(own_states, kinds_row, blocks, 0, count_here)
    cut_tiles = jnp.zeros((TILES_DEV, inst_here, TSIZE), jnp.float32).at[index_row].add(results)
    cut = (
        cut_tiles.reshape(TILES_DEV, inst_here, NVAR, TILE)
        .transpose(1, 2, 0, 3)
        .reshape(inst_here, NVAR, rows_here, row_cells)
    )
    residual = transport + smoothing + cut + timewise
    new_state = state - time_step[None, None] * residual
    return (residual, new_state)


def solution(mesh):
    placed = (
        P(("group", "inst"), None, "brick", None),
        P(("group", "brick"), None),
        P(),
        P("group"),
        P(("group", "brick"), None),
        P(("group", "brick"), None),
    )
    return jax.shard_map(
        per_device,
        mesh=mesh,
        in_specs=placed,
        out_specs=(
            P(("group", "inst"), None, "brick", None),
            P(("group", "inst"), None, "brick", None),
        ),
        check_vma=False,
    )
```

profile of v0, /device:TPU:0, one launch (start us, length us, event | category | flops | bytes accessed | tf_op | source)
XLA Modules:
  0.0 146.6 jit_solution(6179582172153618926)
XLA Ops:
  7.2 0.0 copy-start.1
  7.2 0.0 all-gather.2.cloned.1.call-start
  7.2 0.7 all-gather.2.cloned.1.call-update
  7.9 1.0 copy-done.1
  8.9 1.7 %copy.75 = bf16[4,5,8,4096]{3,0,2,1:T(4,128)(2,1)S(1)} copy(f32[4,5,8,4096]{3,2,1,0:T(8,128)S(1)} %copy-done.1) | data formatting | bytes 3932160 | tf_op args[0]
  10.6 0.0 copy-start.2
  10.6 1.0 copy-done.2
  11.7 1.1 fusion.82
  12.8 5.6 %collective-permute-start = (bf16[4,5,2,4096]{3,0,2,1:T(4,128)(2,1)}, bf16[4,5,2,4096]{3,0,2,1:T(4,128)(2,1)}, u32[]{:S(2)}, u32[]{:S(2)}) collective-permute-start(bf16[4,5,2,4096]{3,0,2,1:T(4,128)(2,1)} %get-tuple-element.19), channel_id=1, source_target_pairs={{0,1},{1,2},{2,3},{4,5},{5,6},{6,7},{8,9},{9,10},{10,11},{12,13},{... | collective-permute-start | bytes 983048 | tf_op jit(solution)/shard_map/ppermute | solution.py:25
  18.4 1.5 collective-permute-start.1
  19.9 3.5 %reshape.131 = bf16[4,5,512,64]{3,2,1,0:T(8,128)(2,1)} reshape(f32[4,5,8,4096]{3,2,1,0:T(8,128)S(1)} %copy-done.1) | data formatting | bytes 3932160 | tf_op jit(solution)/shard_map/reshape | solution.py:99
  23.4 0.0 copy-start.7
  23.4 0.0 copy-start.5
  23.4 4.3 %copy.33 = bf16[512,4,5,64]{0,3,2,1:T(8,128)(2,1)} copy(bf16[512,4,5,64]{3,0,2,1:T(8,128)(2,1)} %bitcast.52) | data formatting | bytes 2621440 | tf_op jit(solution)/shard_map/transpose | solution.py:100
  27.7 0.0 copy-start.4
  27.7 3.5 %copy.34 = bf16[512,4,320]{2,1,0:T(4,128)(2,1)} copy(bf16[512,4,320]{0,2,1:T(8,128)(2,1)} %bitcast.54) | data formatting | bytes 2621440 | tf_op jit(solution)/shard_map/reshape | solution.py:101
  31.2 0.0 copy-done.7
  31.3 0.6 dynamic_slice.3
  31.8 0.0 copy-done.5
  31.8 3.0 %gather_fusion = bf16[256,4,320]{2,1,0:T(4,128)(2,1)S(1)} fusion(bf16[512,4,320]{2,1,0:T(4,128)(2,1)} %copy.34, s32[1024]{0:T(1024)S(1)} %pad_clamp_fusion), kind=kCustom, calls=%fused_computation | custom fusion | bytes 1311744 | tf_op jit(solution)/shard_map/gather | solution.py:105
  34.8 0.0 copy-done.4
  34.9 0.7 fusion.64
  35.5 0.7 fusion.66
  36.2 0.7 fusion.68
  36.9 0.7 fusion.70
  37.5 0.0 copy-start.3
  37.5 4.3 %broadcast_select_fusion = (bf16[256,4,320]{2,1,0:T(4,128)(2,1)S(1)}, bf16[256,4,320]{2,1,0:T(4,128)(2,1)S(1)}, bf16[256,4,320]{2,1,0:T(4,128)(2,1)S(1)}, bf16[2...) fusion(bf16[256,4,320]{2,1,0:T(4,128)(2,1)S(1)} %gather_fusion,, ...), kind=kLoop, calls=%fused_computation.42 | loop fusion | flops 2621440 | bytes 5900288 | tf_op jit(solution)/shard_map/jit(_where)/select_n | solution.py:72
  41.9 0.0 copy-done.3
  41.9 0.5 fusion.19
  42.4 0.5 convolution_add_fusion.6
  43.0 0.5 convolution_add_fusion.5
  43.5 0.5 convolution_add_fusion.4
  44.1 0.5 convolution_add_fusion.3
  44.6 0.5 convolution_add_fusion.2
  45.2 0.5 convolution_add_fusion.1
  45.7 1.6 %convolution_add_fusion = f32[256,4,320]{0,2,1:T(8,128)} fusion(f32[256,4,320]{0,2,1:T(8,128)S(1)} %convolution_add_fusion.1, bf16[256,4,320]{2,1,0:T(4,128)(2,1)S(1)} %get-tuple-element.21, bf16[8,320,320]{2,1,0:T(8,128)(2,1)S(1)} %copy-done.3), kind=kOutput, calls=%fused_computation.21 | convolution fusion | flops 210042880 | bytes 3653632 | tf_op jit(solution)/shard_map/ab,tib->tia/dot_general | solution.py:73
  47.3 2.5 %copy.43 = f32[256,4,320]{2,1,0:T(4,128)} copy(f32[256,4,320]{0,2,1:T(8,128)} %convolution_add_fusion) | data formatting | bytes 2621440 | tf_op jit(solution)/shard_map/add | solution.py:73
  49.8 2.2 %broadcast_in_dim.70 = f32[512,4,320]{2,1,0:T(4,128)} broadcast(f32[]{:T(128)} %constant.23.clone.1), dimensions={} | broadcast | bytes 2621444 | tf_op jit(solution)/shard_map/broadcast_in_dim | solution.py:109
  52.0 32.5 %scatter_fusion = f32[512,4,320]{2,1,0:T(4,128)} fusion(f32[512,4,320]{2,1,0:T(4,128)} %broadcast_in_dim.70, s32[256]{0:T(256)S(1)} %bitcast.56, f32[256,4,320]{2,1,0:T(4,128)} %copy.43), kind=kCustom, calls=%fused_computation.1 | custom fusion | flops 327680 | bytes 3933184 | tf_op jit(solution)/shard_map/scatter-add | solution.py:109
  84.5 4.7 %copy.44 = f32[512,4,320]{0,2,1:T(8,128)} copy(f32[512,4,320]{2,1,0:T(4,128)} %scatter_fusion) | data formatting | bytes 5242880 | tf_op jit(solution)/shard_map/scatter-add | solution.py:109
  89.2 4.9 %copy.45 = f32[4,5,512,64]{3,2,1,0:T(8,128)} copy(f32[4,5,512,64]{2,3,1,0:T(8,128)} %bitcast.53) | data formatting | bytes 5242880 | tf_op jit(solution)/shard_map/transpose | solution.py:112
  94.0 5.4 %reshape.134 = f32[4,5,8,4096]{3,2,1,0:T(8,128)} reshape(f32[4,5,512,64]{3,2,1,0:T(8,128)} %copy.45) | data formatting | bytes 5242880 | tf_op jit(solution)/shard_map/reshape | solution.py:113
  99.4 0.0 collective-permute-done
  99.4 0.0 collective-permute-done.1
  99.4 2.5 %maximum_convert_fusion = f32[4,5,12,4096]{3,0,2,1:T(4,128)S(1)} fusion(bf16[4,5,2,4096]{3,0,2,1:T(4,128)(2,1)} %collective-permute-done.1, bf16[4,5,8,4096]{3,0,2,1:T(4,128)(2,1)} %copy-done.2, bf16[4,5,2,4096]{3,0,2,1:T(4,128)(2,1)} %collective-permute-done), kind=kLoop, calls=%fused_computation.20 | loop fusion | flops 2949120 | bytes 5898240 | tf_op jit(solution)/shard_map/convert_element_type | solution.py:83
  101.9 0.0 copy-start
  102.0 1.0 slice_dynamic-update-slice_fusion
  103.0 1.9 %add_dynamic-update-slice_fusion = (f32[4,5,12,4096]{3,0,2,1:T(4,128)}, f32[4,1,12,4096]{3,0,2,1:T(4,128)S(1)}, f32[4,1,12,4096]{3,0,2,1:T(4,128)S(1)}) fusion(f32[4,5,12,4096]{3,0,2,1:T(4,128)} %slice_dynamic-update-slice_fusion, f32[4,5,12,4096]{3,0,2,1:T(4,128)S(1)} %maximum_convert_fusion), kind=kLoop, calls=%fused_computation.40 | loop fusion | flops 2752512 | bytes 6291456
  104.9 1.1 multiply_dynamic-update-slice_fusion.2
  106.0 0.0 copy-start.6
  106.0 1.1 multiply_dynamic-update-slice_fusion.1
  107.1 0.0 copy-done
  107.1 1.2 multiply_dynamic-update-slice_fusion
  108.3 0.0 all-gather.2.cloned.1.call-done
  108.3 0.0 copy-done.6
  108.3 25.4 %multiply_subtract_fusion = (f32[4,5,8,4096]{3,0,2,1:T(4,128)S(1)}, f32[4,5,8,4096]{3,0,2,1:T(4,128)S(1)}) fusion(f32[4,5,8,4096]{3,2,1,0:T(8,128)S(1)} %copy-done.1, f32[8,4096]{1,0:T(8,128)S(1)} %copy-done.6, f32[16,5,8,4096]{3,2,1,0:T(8,128)} %all-gather.2.cloned.1.call-done, s32[4]{0:T(128)S(1)} %iota_add_fusion, f32[4,5,8,4096]{3,2,1,0:T(8,128)} %reshape.134, ...), kind=kOutput, calls=%fused_computation.17 | convolution fusion | flops 135661376 | bytes 39452688 | tf_op jit(solution)/shard_map/jk,kcxs->jcxs/dot_general | solution.py:97
  133.7 3.0 %copy.49 = f32[4,5,8,4096]{3,2,1,0:T(8,128)} copy(f32[4,5,8,4096]{3,0,2,1:T(4,128)S(1)} %get-tuple-element.30) | data formatting | bytes 5242880
  136.7 3.0 %copy.50 = f32[4,5,8,4096]{3,2,1,0:T(8,128)} copy(f32[4,5,8,4096]{3,0,2,1:T(4,128)S(1)} %get-tuple-element.29) | data formatting | bytes 5242880
  (4 shorter events, 0.1 us)
Async XLA Ops:
  7.2 1.7 %copy-start.1 = (f32[4,5,8,4096]{3,2,1,0:T(8,128)S(1)}, f32[4,5,8,4096]{3,2,1,0:T(8,128)}, u32[]{:S(2)}) copy-start(f32[4,5,8,4096]{3,2,1,0:T(8,128)} %param.6) | copy-start | bytes 7864324
  7.2 101.1 %all-gather.2.cloned.1.call-start = ((), (), s32[]{:S(2)}) async-start(), calls=%async_computation | async-start | bytes 13107200 | tf_op jit(solution)/shard_map/all_gather | solution.py:94
  10.6 1.1 copy-start.2
  12.8 86.6 %collective-permute-start = (bf16[4,5,2,4096]{3,0,2,1:T(4,128)(2,1)}, bf16[4,5,2,4096]{3,0,2,1:T(4,128)(2,1)}, u32[]{:S(2)}, u32[]{:S(2)}) collective-permute-start(bf16[4,5,2,4096]{3,0,2,1:T(4,128)(2,1)} %get-tuple-element.19), channel_id=1, source_target_pairs={{0,1},{1,2},{2,3},{4,5},{5,6},{6,7},{8,9},{9,10},{10,11},{12,13},{... | collective-permute-start | bytes 983048 | tf_op jit(solution)/shard_map/ppermute | solution.py:25
  18.4 81.0 %collective-permute-start.1 = (bf16[4,5,2,4096]{3,0,2,1:T(4,128)(2,1)}, bf16[4,5,2,4096]{3,0,2,1:T(4,128)(2,1)}, u32[]{:S(2)}, u32[]{:S(2)}) collective-permute-start(bf16[4,5,2,4096]{3,0,2,1:T(4,128)(2,1)} %get-tuple-element.20), channel_id=1, source_target_pairs={{1,0},{2,1},{3,2},{5,4},{6,5},{7,6},{9,8},{10,9},{11,10},{13,12},{... | collective-permute-start | bytes 983048 | tf_op jit(solution)/shard_map/ppermute | solution.py:27
  23.4 7.9 %copy-start.7 = (s32[4]{0:T(128)S(1)}, s32[4]{0:T(128)}, u32[]{:S(2)}) copy-start(s32[4]{0:T(128)} %param.9) | copy-start | bytes 52
  23.4 8.4 %copy-start.5 = (s32[1,256]{1,0:T(1,128)S(1)}, s32[1,256]{1,0:T(1,128)}, u32[]{:S(2)}) copy-start(s32[1,256]{1,0:T(1,128)} %param.10) | copy-start | bytes 3076
  27.7 7.1 %copy-start.4 = (s32[1,256]{1,0:T(1,128)S(1)}, s32[1,256]{1,0:T(1,128)}, u32[]{:S(2)}) copy-start(s32[1,256]{1,0:T(1,128)} %param.11) | copy-start | bytes 3076
  37.5 4.4 %copy-start.3 = (bf16[8,320,320]{2,1,0:T(8,128)(2,1)S(1)}, bf16[8,320,320]{2,1,0:T(8,128)(2,1)}, u32[]{:S(2)}) copy-start(bf16[8,320,320]{2,1,0:T(8,128)(2,1)} %param.8) | copy-start | bytes 4915204
  101.9 5.1 %copy-start = (f32[4,5,12,4096]{3,0,2,1:T(4,128)}, f32[4,5,12,4096]{3,0,2,1:T(4,128)S(1)}, u32[]{:S(2)}) copy-start(f32[4,5,12,4096]{3,0,2,1:T(4,128)S(1)} %maximum_convert_fusion) | copy-start | bytes 11796484
  106.0 2.3 %copy-start.6 = (f32[8,4096]{1,0:T(8,128)S(1)}, f32[8,4096]{1,0:T(8,128)}, u32[]{:S(2)}) copy-start(f32[8,4096]{1,0:T(8,128)} %param.7) | copy-start | bytes 393220
Sparse Core Ops, SparseCore 0:
  9.6 72.8 all-gather.1
where the time goes:
time: 148 us; the launch traced here: 147 us
  other arithmetic  47.3 us (32%)
  local copies, waits for them, and re-layouts  46.4 us (31%)
  matrix products  30.8 us (21%)
  between operations  14.2 us (10%)
  starting transfers between devices  7.15 us (5%)
    scatter-add x1, other arithmetic, per_device(): jnp.zeros((TILES_DEV, inst_here, TSIZE), jnp.float32).at[index_row]  32.5 us
    dot_general x1, matrix products, per_device(): jnp.einsum('jk,kcxs->jcxs', coef, piece, precision=lax.Precision.HIGHEST)  25.4 us
    unnamed x20, local copies, waits for them, and re-layouts  10.8 us
    ppermute x1, starting transfers between devices, padded(): lax.ppermute(tail, axis, [(i, (i + 1) % count) for i in range(ends)])  5.65 us
    reshape x1, local copies, waits for them, and re-layouts, per_device(): cut = cut_tiles.reshape(TILES_DEV, inst_here, NVAR, TILE).transpose(1, 2,...  5.37 us
    dot_general x8, matrix products, apply_range(): jnp.einsum('ab,tib->tia', blocks[kind], masked, preferred_element_type=jn...  5.37 us
    transpose x1, local copies, waits for them, and re-layouts, per_device(): cut = cut_tiles.reshape(TILES_DEV, inst_here, NVAR, TILE).transpose(1, 2,...  4.86 us
    scatter-add x1, local copies, waits for them, and re-layouts, per_device(): jnp.zeros((TILES_DEV, inst_here, TSIZE), jnp.float32).at[index_row]  4.68 us
  transfers between devices with their start and end apart: 3, of which 0 were waited for; matrix products, arithmetic and copies ran while one was open for 62% of the time, Pallas kernels for 0%

commit v1 on v0

v1 whole, which is shorter than its diff:
```python
import functools
import math

import jax
import jax.numpy as jnp
from jax import lax
from jax.experimental import pallas as pl
from jax.experimental.pallas import tpu as pltpu
from jax.sharding import PartitionSpec as P

MESH = pl.DeviceIdType.MESH
GAMMA_MINUS = 0.4
EPS_FOURTH = 0.03125
CENTRE = (1.25, 0.0, 0.0, 0.0, 2.75)
LANES = 128


def spectral(m, count):
    m = m % count
    if m == 0 or 2 * m == count:
        return 0.0
    return (-1.0) ** m / math.tan(math.pi * m / count)


def flux_of(q):
    den, one, two, three, energy = q
    inv = 1.0 / den
    speed = one * inv
    press = GAMMA_MINUS * (energy - 0.5 * (one * one + two * two + three * three) * inv)
    return (one, one * speed + press, two * speed, three * speed, (energy + press) * speed)


def kernel(
    sizes, state, step, blocks, counts, index, kinds, res_out, new_out,
    x, sib, send, cross, fwd, halo_out, halo_in, wide, xs, lhs, km, acc, fresh,
    in_sem, sib_send, sib_recv, cross_send, cross_recv, fwd_send, fwd_recv, halo_send, halo_recv, out_sem,
):
    inst, nvar, rows, cells, tile, total, chunks, n_brick = sizes
    width = cells // chunks
    ntypes = blocks.shape[0]
    group = lax.axis_index("group")
    me = lax.axis_index("inst")
    brick = lax.axis_index("brick")
    core = lax.rem(me, 2)
    chip = me // 2
    sibling = (group, chip * 2 + (1 - core), brick)
    partner = (group, (1 - chip) * 2 + core, brick)
    below = (group, me, brick - 1)
    above = (group, me, brick + 1)
    has_below = brick > 0
    has_above = brick < n_brick - 1

    def lanes(c):
        return pl.ds(pl.multiple_of(c * width, LANES), width)

    def fetch(c):
        return pltpu.make_async_copy(state.at[:, lanes(c)], x.at[:, lanes(c)], in_sem.at[c])

    def to_sibling(c):
        return pltpu.make_async_remote_copy(
            x.at[:, lanes(c)], sib.at[:, lanes(c)], sib_send.at[c], sib_recv.at[c], sibling, device_id_type=MESH)

    def to_partner(c):
        return pltpu.make_async_remote_copy(
            send.at[c], cross.at[c], cross_send.at[c], cross_recv.at[c], partner, device_id_type=MESH)

    def forward(c):
        return pltpu.make_async_remote_copy(
            cross.at[c], fwd.at[c], fwd_send.at[c], fwd_recv.at[c], sibling, device_id_type=MESH)

    def halo(side):
        return pltpu.make_async_remote_copy(
            halo_out.at[side], halo_in.at[side], halo_send.at[side], halo_recv.at[side],
            below if side == 0 else above, device_id_type=MESH)

    @pl.loop(0, chunks)
    def _(c):
        fetch(c).start()

    barrier = pltpu.get_barrier_semaphore()
    pl.semaphore_signal(barrier, inc=1, device_id=sibling, device_id_type=MESH)
    pl.semaphore_signal(barrier, inc=1, device_id=partner, device_id_type=MESH)

    @pl.when(has_below)
    def _():
        pl.semaphore_signal(barrier, inc=1, device_id=below, device_id_type=MESH)

    @pl.when(has_above)
    def _():
        pl.semaphore_signal(barrier, inc=1, device_id=above, device_id_type=MESH)

    ends = n_brick - 1
    pl.semaphore_wait(barrier, 2 + (brick + ends) // n_brick + (ends - brick + ends) // n_brick)

    @pl.loop(0, chunks)
    def _(c):
        fetch(c).wait()
        for v in range(nvar):
            block = jnp.concatenate(
                [x[(i * nvar + v) * rows:(i * nvar + v + 1) * rows, lanes(c)] for i in range(inst)], axis=0)
            send[c, v * inst * rows:(v + 1) * inst * rows, :] = (block - CENTRE[v]).astype(jnp.bfloat16)
        to_partner(c).start()
        to_sibling(c).start()

    for v in range(nvar):
        for i in range(inst):
            at = (i * nvar + v) * rows
            halo_out[0, v, 2 * i:2 * i + 2, :] = x[at:at + 2, :]
            halo_out[1, v, 2 * i:2 * i + 2, :] = x[at + rows - 2:at + rows, :]

    @pl.when(has_below)
    def _():
        halo(0).start()

    @pl.when(has_above)
    def _():
        halo(1).start()

    per_row = cells // tile
    count = counts[brick]
    slots = index.shape[1]
    where_at = index[...]
    used = lax.broadcasted_iota(jnp.int32, (1, slots), 1) < count
    label = jnp.where(used, kinds[...] + 1, 0).astype(jnp.float32)
    tile_row = where_at // per_row
    tile_col = where_at - tile_row * per_row
    by_row = jnp.where(
        lax.broadcasted_iota(jnp.int32, (rows, slots), 0) == tile_row, label, 0.0).astype(jnp.bfloat16)
    by_col = jnp.where(
        lax.broadcasted_iota(jnp.int32, (per_row, slots), 0) == tile_col, 1.0, 0.0).astype(jnp.bfloat16)
    kind_map = lax.dot_general(
        by_row, by_col, (((1,), (1,)), ((), ())), preferred_element_type=jnp.float32).astype(jnp.bfloat16)
    spread = jnp.where(
        lax.broadcasted_iota(jnp.int32, (per_row, cells), 1) // tile
        == lax.broadcasted_iota(jnp.int32, (per_row, cells), 0), 1.0, 0.0).astype(jnp.bfloat16)
    kind_cells = jnp.dot(kind_map, spread, preferred_element_type=jnp.float32)

    groups = cells // LANES
    for g in range(groups):
        mask = kind_cells[:, g * LANES:(g + 1) * LANES]
        km[g * inst * rows:(g + 1) * inst * rows, :] = jnp.concatenate([mask] * inst, axis=0)
        for v in range(nvar):
            xs[g * inst * rows:(g + 1) * inst * rows, v * LANES:(v + 1) * LANES] = jnp.concatenate(
                [x[(i * nvar + v) * rows:(i * nvar + v + 1) * rows, g * LANES:(g + 1) * LANES]
                 for i in range(inst)], axis=0).astype(jnp.bfloat16)

    first = lax.broadcasted_iota(jnp.int32, (tile, LANES), 1) < tile

    @pl.loop(0, ntypes)
    def _(k):
        for out in range(nvar):
            for v in range(nvar):
                piece = blocks[k, out * tile:(out + 1) * tile, v * tile:(v + 1) * tile].astype(jnp.float32)
                both = jnp.concatenate([piece, piece], axis=1)
                at = out * LANES
                wide[k, at:at + tile, v * LANES:(v + 1) * LANES] = jnp.where(first, both, 0.0).astype(jnp.bfloat16)
                wide[k, at + tile:at + LANES, v * LANES:(v + 1) * LANES] = jnp.where(
                    first, 0.0, both).astype(jnp.bfloat16)

    parts = lhs.shape[0]
    depth = nvar * LANES

    @pl.loop(0, groups * inst * rows // parts)
    def _(m):
        at = pl.ds(pl.multiple_of(m * parts, parts), parts)
        kind_here = km[at, :]
        part = jnp.zeros((parts, depth), jnp.float32)
        for k in range(ntypes):
            keep = jnp.where(kind_here == k + 1.0, 1.0, 0.0).astype(jnp.bfloat16)
            for v in range(nvar):
                lhs[:, v * LANES:(v + 1) * LANES] = xs[at, v * LANES:(v + 1) * LANES] * keep
            part = part + lax.dot_general(
                lhs[...], wide[k], (((1,), (1,)), ((), ())), preferred_element_type=jnp.float32)
        per = parts // (inst * rows)
        for g in range(per):
            to = pl.ds(pl.multiple_of((m * per + g) * LANES, LANES), LANES)
            for i in range(inst):
                for v in range(nvar):
                    acc[(i * nvar + v) * rows:(i * nvar + v + 1) * rows, to] = part[
                        (g * inst + i) * rows:(g * inst + i + 1) * rows, v * LANES:(v + 1) * LANES]

    @pl.when(has_below)
    def _():
        halo(0).wait_send()
        halo(1).wait_recv()

    @pl.when(has_above)
    def _():
        halo(1).wait_send()
        halo(0).wait_recv()

    @pl.when(jnp.logical_not(has_below))
    def _():
        halo_in[1] = jnp.zeros(halo_in.shape[1:], jnp.float32)

    @pl.when(jnp.logical_not(has_above))
    def _():
        halo_in[0] = jnp.zeros(halo_in.shape[1:], jnp.float32)

    near = LANES

    @pl.loop(0, cells // near)
    def _(b):
        at = pl.ds(pl.multiple_of(b * near, LANES), near)
        for i in range(inst):
            full = []
            for v in range(nvar):
                full.append(jnp.concatenate([
                    halo_in[1, v, 2 * i:2 * i + 2, at],
                    x[(i * nvar + v) * rows:(i * nvar + v + 1) * rows, at],
                    halo_in[0, v, 2 * i:2 * i + 2, at],
                ], axis=0))
            safe = [jnp.where(full[0] == 0.0, 1.0, full[0])] + full[1:]
            flux = flux_of(safe)
            for v in range(nvar):
                q, f = full[v], flux[v]
                put = slice((i * nvar + v) * rows, (i * nvar + v + 1) * rows)
                acc[put, at] = acc[put, at] + 0.5 * (f[3:rows + 3] - f[1:rows + 1]) + EPS_FOURTH * (
                    q[4:] - 4.0 * q[3:-1] + 6.0 * q[2:-2] - 4.0 * q[1:-3] + q[:-4])

    def choose(a, b):
        return a if a == b else jnp.where(core == 0, a, b)

    span = range(1 - inst, inst)
    half = total // 2
    d_own = {m: spectral(m, total) for m in span}
    d_sib = {m: choose(spectral(m - inst, total), spectral(m + inst, total)) for m in span}
    d_cross = {m: spectral(m - half, total) for m in span}
    d_fwd = {m: choose(spectral(m - inst - half, total), spectral(m + inst - half, total)) for m in span}

    def finish(c):
        at = lanes(c)
        for v in range(nvar):
            cut = slice(v * inst * rows, (v + 1) * inst * rows)
            one = cross[c, cut, :].astype(jnp.float32)
            two = fwd[c, cut, :].astype(jnp.float32)
            for j in range(inst):
                put = slice((j * nvar + v) * rows, (j * nvar + v + 1) * rows)
                value = acc[put, at]
                for k in range(inst):
                    take = slice((k * nvar + v) * rows, (k * nvar + v + 1) * rows)
                    local = slice(k * rows, (k + 1) * rows)
                    m = j - k
                    if m:
                        value = value + d_own[m] * (x[take, at] - CENTRE[v])
                        value = value + d_cross[m] * one[local]
                    value = value + d_sib[m] * (sib[take, at] - CENTRE[v])
                    value = value + d_fwd[m] * two[local]
                acc[put, at] = value
                fresh[put, at] = x[put, at] - step[:, at] * value
        pltpu.make_async_copy(acc.at[:, at], res_out.at[:, at], out_sem.at[0, c]).start()
        pltpu.make_async_copy(fresh.at[:, at], new_out.at[:, at], out_sem.at[1, c]).start()

    @pl.loop(0, chunks)
    def _(c):
        to_sibling(c).wait()
        to_partner(c).wait()
        forward(c).start()

        @pl.when(c > 0)
        def _():
            forward(c - 1).wait()
            finish(c - 1)

    forward(chunks - 1).wait()
    finish(chunks - 1)

    @pl.loop(0, chunks)
    def _(c):
        at = lanes(c)
        pltpu.make_async_copy(acc.at[:, at], res_out.at[:, at], out_sem.at[0, c]).wait()
        pltpu.make_async_copy(fresh.at[:, at], new_out.at[:, at], out_sem.at[1, c]).wait()


def fused(mesh, state, time_step, blocks, cut_counts, tile_index, tile_type):
    inst, nvar, rows, cells = state.shape
    tile = blocks.shape[1] // nvar
    total = inst * mesh.shape["inst"]
    n_brick = mesh.shape["brick"]
    chunks = 8
    all_rows = inst * nvar * rows
    width = cells // chunks
    depth = nvar * LANES
    product_rows = cells // LANES * inst * rows
    sizes = (inst, nvar, rows, cells, tile, total, chunks, n_brick)
    vmem = pl.BlockSpec(memory_space=pltpu.VMEM)
    hbm = pl.BlockSpec(memory_space=pl.ANY)
    dma = pltpu.SemaphoreType.DMA
    flat = state.reshape(all_rows, cells)
    res, new = pl.pallas_call(
        functools.partial(kernel, sizes),
        out_shape=[jax.ShapeDtypeStruct(flat.shape, jnp.float32)] * 2,
        in_specs=[hbm, vmem, vmem, pl.BlockSpec(memory_space=pltpu.SMEM), vmem, vmem],
        out_specs=[hbm, hbm],
        scratch_shapes=[
            pltpu.VMEM((all_rows, cells), jnp.float32),
            pltpu.VMEM((all_rows, cells), jnp.float32),
            pltpu.VMEM((chunks, all_rows, width), jnp.bfloat16),
            pltpu.VMEM((chunks, all_rows, width), jnp.bfloat16),
            pltpu.VMEM((chunks, all_rows, width), jnp.bfloat16),
            pltpu.VMEM((2, nvar, 2 * inst, cells), jnp.float32),
            pltpu.VMEM((2, nvar, 2 * inst, cells), jnp.float32),
            pltpu.VMEM((blocks.shape[0], depth, depth), jnp.bfloat16),
            pltpu.VMEM((product_rows, depth), jnp.bfloat16),
            pltpu.VMEM((min(256, product_rows), depth), jnp.bfloat16),
            pltpu.VMEM((product_rows, LANES), jnp.float32),
            pltpu.VMEM((all_rows, cells), jnp.float32),
            pltpu.VMEM((all_rows, cells), jnp.float32),
            dma((chunks,)), dma((chunks,)), dma((chunks,)), dma((chunks,)), dma((chunks,)),
            dma((chunks,)), dma((chunks,)), dma((2,)), dma((2,)), dma((2, chunks)),
        ],
        compiler_params=pltpu.CompilerParams(
            collective_id=0, has_side_effects=True, vmem_limit_bytes=48 * 1024 * 1024),
        cost_estimate=pl.CostEstimate(
            flops=2 * product_rows * depth * depth * blocks.shape[0], bytes_accessed=12 * all_rows * cells,
            transcendentals=0),
    )(flat, time_step, blocks, cut_counts, tile_index, tile_type)
    return res.reshape(state.shape), new.reshape(state.shape)


def plain(mesh, state, time_step, blocks, cut_counts, tile_index, tile_type):
    inst, nvar, rows, cells = state.shape
    tile = blocks.shape[1] // nvar
    size = mesh.shape["inst"]
    total = inst * size
    ends = mesh.shape["brick"] - 1
    tail = lax.ppermute(state[:, :, rows - 2:], "brick", [(i, i + 1) for i in range(ends)])
    head = lax.ppermute(state[:, :, :2], "brick", [(i + 1, i) for i in range(ends)])
    q = jnp.concatenate([tail, state, head], axis=2)
    density = jnp.where(q[:, 0] == 0.0, 1.0, q[:, 0])
    f = jnp.stack(flux_of((density, q[:, 1], q[:, 2], q[:, 3], q[:, 4])), axis=1)
    local = 0.5 * (f[:, :, 3:-1] - f[:, :, 1:-3]) + EPS_FOURTH * (
        q[:, :, 4:] - 4.0 * q[:, :, 3:-1] + 6.0 * q[:, :, 2:-2] - 4.0 * q[:, :, 1:-3] + q[:, :, :-4])
    table = jnp.asarray([spectral(m, total) for m in range(total)], jnp.float32)
    mine = lax.axis_index("inst") * inst + jnp.arange(inst)
    timewise = jnp.zeros(state.shape, jnp.float32)
    moving = state
    for hop in range(size):
        source = lax.rem(lax.axis_index("inst") + size - hop, size) * inst + jnp.arange(inst)
        coef = table[jnp.mod(mine[:, None] - source[None, :], total)]
        timewise = timewise + jnp.einsum("jk,kcxs->jcxs", coef, moving, precision=lax.Precision.HIGHEST)
        if hop < size - 1:
            moving = lax.ppermute(moving, "inst", [(i, (i + 1) % size) for i in range(size)])
    tiles = rows * cells // tile
    slots = jnp.arange(tile_index.shape[1])
    used = slots < cut_counts[lax.axis_index("brick")]
    label = jnp.where(used, tile_type[0], blocks.shape[0])
    hot = (tile_index[0][None, :] == jnp.arange(tiles)[:, None]) & used[None, :]
    kind = jnp.where(jnp.any(hot, axis=1), jnp.sum(jnp.where(hot, label[None, :], 0), axis=1), blocks.shape[0])
    by_tile = state.reshape(inst, nvar, tiles, tile).transpose(2, 0, 1, 3).reshape(tiles, inst, nvar * tile)
    by_tile = by_tile.astype(jnp.bfloat16)
    cut = jnp.zeros(by_tile.shape, jnp.float32)
    for k in range(blocks.shape[0]):
        masked = jnp.where((kind == k)[:, None, None], by_tile, jnp.zeros_like(by_tile))
        cut = cut + jnp.einsum("ab,tib->tia", blocks[k], masked, preferred_element_type=jnp.float32)
    cut = cut.reshape(tiles, inst, nvar, tile).transpose(1, 2, 0, 3).reshape(state.shape)
    residual = local + cut + timewise
    return residual, state - time_step[None, None] * residual


def solution(mesh):
    placed = (
        P(("group", "inst"), None, "brick", None),
        P(("group", "brick"), None),
        P(),
        P("group"),
        P(("group", "brick"), None),
        P(("group", "brick"), None),
    )
    body = fused if mesh.shape["inst"] == 4 else plain
    return jax.shard_map(
        functools.partial(body, mesh),
        mesh=mesh,
        in_specs=placed,
        out_specs=(
            P(("group", "inst"), None, "brick", None),
            P(("group", "inst"), None, "brick", None),
        ),
        check_vma=False,
    )
```

time: 148 us -> 46.1 us (0.31)
  other arithmetic: 47.3 us -> 0 us
  local copies, waits for them, and re-layouts: 46.4 us -> 8.62 us
  Pallas kernels: 0 us -> 36.5 us
  matrix products: 30.8 us -> 0 us
  between operations: 14.2 us -> 0.66 us
  starting transfers between devices: 7.15 us -> 0 us
    pallas_call x0 -> x1, Pallas kernels: none -> 36.5 us  [fused(): pl.pallas_call(functools.partial(kernel, sizes), out_shape=[jax.ShapeDtyp...]
    scatter-add x1 -> x0, other arithmetic: 32.5 us -> none  [per_device(): jnp.zeros((TILES_DEV, inst_here, TSIZE), jnp.float32).at[index_row]]
    dot_general x9 -> x0, matrix products: 30.8 us -> none  [the longest x1 25.4 us: per_device(): jnp.einsum('jk,kcxs->jcxs', coef, piece, precision=lax.Precision.HIGHEST)]
    reshape x3 -> x0, local copies, waits for them, and re-layouts: 12.4 us -> none  [the longest x1 5.37 us: per_device(): cut = cut_tiles.reshape(TILES_DEV, inst_here, NVAR, TILE).transpose(1, 2,...]
    transpose x2 -> x0, local copies, waits for them, and re-layouts: 9.16 us -> none  [the longest x1 4.86 us: per_device(): cut = cut_tiles.reshape(TILES_DEV, inst_here, NVAR, TILE).transpose(1, 2,...]
    ppermute x2 -> x0, starting transfers between devices: 7.11 us -> none  [the longest x1 5.65 us: padded(): lax.ppermute(tail, axis, [(i, (i + 1) % count) for i in range(ends)])]
    scatter-add x1 -> x0, local copies, waits for them, and re-layouts: 4.68 us -> none  [per_device(): jnp.zeros((TILES_DEV, inst_here, TSIZE), jnp.float32).at[index_row]]
    select_n x2 -> x0, other arithmetic: 4.33 us -> none  [the longest x1 4.33 us: apply_range(): masked = jnp.where(select[:, None, None], states, jnp.zeros_like(states))]
  transfers between devices with their start and end apart: 3 -> 0, of which waited for: 0 -> 0; matrix products, arithmetic and copies ran while one was open for 62% -> 0% of each run, Pallas kernels for 0% -> 0%
where the time goes in v1:
time: 46.1 us; the launch traced here: 45.8 us
  Pallas kernels  36.5 us (79%)
  local copies, waits for them, and re-layouts  8.62 us (19%)
  between operations  0.66 us (1%)
    pallas_call x1, Pallas kernels, fused(): pl.pallas_call(functools.partial(kernel, sizes), out_shape=[jax.ShapeDtyp...  36.5 us
    unnamed x14, local copies, waits for them, and re-layouts  8.62 us

profile of v1, /device:TPU:0, one launch (start us, length us, event | category | flops | bytes accessed | tf_op | source)
XLA Modules:
  0.0 45.8 jit_solution(14189181748108156548)
XLA Ops:
  0.6 0.0 copy-start
  0.6 1.5 %copy-done = bf16[8,320,320]{2,1,0:T(8,128)(2,1)S(1)} copy-done((bf16[8,320,320]{2,1,0:T(8,128)(2,1)S(1)}, bf16[8,320,320]{2,1,0:T(8,128)(2,1)}, u32[]{:S(2)}) %copy-start) | copy-done | bytes 1638424
  2.2 0.0 copy-start.1
  2.2 0.9 %copy-done.1 = f32[8,4096]{1,0:T(8,128)S(1)} copy-done((f32[8,4096]{1,0:T(8,128)S(1)}, f32[8,4096]{1,0:T(8,128)}, u32[]{:S(2)}) %copy-start.1) | copy-done | bytes 131096
  3.1 0.0 copy-start.2
  3.1 0.7 %copy-done.2 = s32[1,256]{1,0:T(1,128)S(1)} copy-done((s32[1,256]{1,0:T(1,128)S(1)}, s32[1,256]{1,0:T(1,128)}, u32[]{:S(2)}) %copy-start.2) | copy-done | bytes 1048
  3.8 0.0 copy-start.3
  3.8 0.7 %copy-done.3 = s32[1,256]{1,0:T(1,128)S(1)} copy-done((s32[1,256]{1,0:T(1,128)S(1)}, s32[1,256]{1,0:T(1,128)}, u32[]{:S(2)}) %copy-start.3) | copy-done | bytes 1048
  4.4 0.0 copy-start.4
  4.4 0.7 %copy-done.4 = s32[4]{0:T(128)S(1)} copy-done((s32[4]{0:T(128)S(1)}, s32[4]{0:T(128)}, u32[]{:S(2)}) %copy-start.4) | copy-done | bytes 40
  5.1 36.5 %shard_map.77 = (f32[160,4096]{1,0:T(8,128)S(1)}, f32[160,4096]{1,0:T(8,128)}) custom-call(f32[160,4096]{1,0:T(8,128)} %bitcast.5, f32[8,4096]{1,0:T(8,128)S(1)} %copy-done.1, bf16[8,320,320]{2,1,0:T(8,128)(2,1)S(1)} %copy-done, s32[4]{0:T(128)S(1)} %copy-done.4, s32[1,256]{1,0:T(1,128)S(1)} %copy-done.2, s32[1,256]{1,0:T(1,128)S(1)} %copy-done.3), custom_call_target="tpu_custom_call" | custom-call | flops 6710886400 | bytes 7864320 | tf_op jit(solution)/shard_map/pallas_call | solution.py:290
  41.6 0.0 copy-start.5
  41.6 1.5 %copy.10 = f32[4,5,8,4096]{3,2,1,0:T(8,128)} copy(f32[4,5,8,4096]{3,2,1,0:T(8,128)S(1)} %bitcast.3) | data formatting | bytes 5242880
  43.1 1.2 %copy-done.5 = f32[160,4096]{1,0:T(8,128)S(1)} copy-done((f32[160,4096]{1,0:T(8,128)S(1)}, f32[160,4096]{1,0:T(8,128)}, u32[]{:S(2)}) %copy-start.5) | copy-done | bytes 2621464
  44.3 1.5 %copy.11 = f32[4,5,8,4096]{3,2,1,0:T(8,128)} copy(f32[4,5,8,4096]{3,2,1,0:T(8,128)S(1)} %bitcast.4) | data formatting | bytes 5242880
Async XLA Ops:
  0.6 1.5 %copy-start = (bf16[8,320,320]{2,1,0:T(8,128)(2,1)S(1)}, bf16[8,320,320]{2,1,0:T(8,128)(2,1)}, u32[]{:S(2)}) copy-start(bf16[8,320,320]{2,1,0:T(8,128)(2,1)} %blocks.1) | copy-start | bytes 4915204
  2.2 0.9 %copy-start.1 = (f32[8,4096]{1,0:T(8,128)S(1)}, f32[8,4096]{1,0:T(8,128)}, u32[]{:S(2)}) copy-start(f32[8,4096]{1,0:T(8,128)} %step.1) | copy-start | bytes 393220
  3.1 0.7 %copy-start.2 = (s32[1,256]{1,0:T(1,128)S(1)}, s32[1,256]{1,0:T(1,128)}, u32[]{:S(2)}) copy-start(s32[1,256]{1,0:T(1,128)} %index.1) | copy-start | bytes 3076
  3.8 0.7 %copy-start.3 = (s32[1,256]{1,0:T(1,128)S(1)}, s32[1,256]{1,0:T(1,128)}, u32[]{:S(2)}) copy-start(s32[1,256]{1,0:T(1,128)} %kinds.1) | copy-start | bytes 3076
  4.4 0.7 %copy-start.4 = (s32[4]{0:T(128)S(1)}, s32[4]{0:T(128)}, u32[]{:S(2)}) copy-start(s32[4]{0:T(128)} %counts.1) | copy-start | bytes 52
  41.6 2.7 %copy-start.5 = (f32[160,4096]{1,0:T(8,128)S(1)}, f32[160,4096]{1,0:T(8,128)}, u32[]{:S(2)}) copy-start(f32[160,4096]{1,0:T(8,128)} %get-tuple-element.5) | copy-start | bytes 7864324

commit v2 on v1

--- a/solution.py
+++ b/solution.py
@@ -31,9 +31,9 @@
 
 
 def kernel(
-    sizes, state, step, blocks, counts, index, kinds, res_out, new_out,
-    x, sib, send, cross, fwd, halo_out, halo_in, wide, xs, lhs, km, acc, fresh,
-    in_sem, sib_send, sib_recv, cross_send, cross_recv, fwd_send, fwd_recv, halo_send, halo_recv, out_sem,
+    sizes, state, step_in, blocks_in, counts_in, index_in, kinds_in, acc, fresh,
+    x, sib, send, cross, fwd, halo_out, halo_in, wide, xs, lhs, km, step, blocks, counts, index, kinds,
+    in_sem, sib_send, sib_recv, cross_send, cross_recv, fwd_send, fwd_recv, halo_send, halo_recv, side_sem,
 ):
     inst, nvar, rows, cells, tile, total, chunks, n_brick = sizes
     width = cells // chunks
@@ -77,6 +77,14 @@
     def _(c):
         fetch(c).start()
 
+    side = [
+        pltpu.make_async_copy(a, b, side_sem.at[n])
+        for n, (a, b) in enumerate((
+            (counts_in, counts), (index_in, index), (kinds_in, kinds), (blocks_in, blocks), (step_in, step)))
+    ]
+    for copy in side:
+        copy.start()
+
     barrier = pltpu.get_barrier_semaphore()
     pl.semaphore_signal(barrier, inc=1, device_id=sibling, device_id_type=MESH)
     pl.semaphore_signal(barrier, inc=1, device_id=partner, device_id_type=MESH)
@@ -116,6 +124,8 @@
     def _():
         halo(1).start()
 
+    for copy in side:
+        copy.wait()
     per_row = cells // tile
     count = counts[brick]
     slots = index.shape[1]
@@ -248,8 +258,6 @@
                     value = value + d_fwd[m] * two[local]
                 acc[put, at] = value
                 fresh[put, at] = x[put, at] - step[:, at] * value
-        pltpu.make_async_copy(acc.at[:, at], res_out.at[:, at], out_sem.at[0, c]).start()
-        pltpu.make_async_copy(fresh.at[:, at], new_out.at[:, at], out_sem.at[1, c]).start()
 
     @pl.loop(0, chunks)
     def _(c):
@@ -265,11 +273,20 @@
     forward(chunks - 1).wait()
     finish(chunks - 1)
 
-    @pl.loop(0, chunks)
-    def _(c):
-        at = lanes(c)
-        pltpu.make_async_copy(acc.at[:, at], res_out.at[:, at], out_sem.at[0, c]).wait()
-        pltpu.make_async_copy(fresh.at[:, at], new_out.at[:, at], out_sem.at[1, c]).wait()
+
+def store(chunks, *refs):
+    count = (len(refs) - 1) // 2
+    sem = refs[-1]
+    copies = []
+    for n in range(count):
+        rows = refs[n].shape[0] // chunks
+        for c in range(chunks):
+            at = pl.ds(c * rows, rows)
+            copies.append(pltpu.make_async_copy(refs[n].at[at], refs[count + n].at[at], sem.at[n, c]))
+    for copy in copies:
+        copy.start()
+    for copy in copies:
+        copy.wait()
 
 
 def fused(mesh, state, time_step, blocks, cut_counts, tile_index, tile_type):
@@ -284,14 +301,15 @@
     product_rows = cells // LANES * inst * rows
     sizes = (inst, nvar, rows, cells, tile, total, chunks, n_brick)
     vmem = pl.BlockSpec(memory_space=pltpu.VMEM)
-    hbm = pl.BlockSpec(memory_space=pl.ANY)
+    hbm = pl.BlockSpec(memory_space=pltpu.HBM)
+    anywhere = pl.BlockSpec(memory_space=pl.ANY)
     dma = pltpu.SemaphoreType.DMA
     flat = state.reshape(all_rows, cells)
     res, new = pl.pallas_call(
         functools.partial(kernel, sizes),
-        out_shape=[jax.ShapeDtypeStruct(flat.shape, jnp.float32)] * 2,
-        in_specs=[hbm, vmem, vmem, pl.BlockSpec(memory_space=pltpu.SMEM), vmem, vmem],
-        out_specs=[hbm, hbm],
+        out_shape=[pltpu.VMEM(flat.shape, jnp.float32)] * 2,
+        in_specs=[hbm] * 6,
+        out_specs=[vmem, vmem],
         scratch_shapes=[
             pltpu.VMEM((all_rows, cells), jnp.float32),
             pltpu.VMEM((all_rows, cells), jnp.float32),
@@ -304,17 +322,29 @@
             pltpu.VMEM((product_rows, depth), jnp.bfloat16),
             pltpu.VMEM((min(256, product_rows), depth), jnp.bfloat16),
             pltpu.VMEM((product_rows, LANES), jnp.float32),
-            pltpu.VMEM((all_rows, cells), jnp.float32),
-            pltpu.VMEM((all_rows, cells), jnp.float32),
+            pltpu.VMEM(time_step.shape, jnp.float32),
+            pltpu.VMEM(blocks.shape, blocks.dtype),
+            pltpu.SMEM(cut_counts.shape, jnp.int32),
+            pltpu.VMEM(tile_index.shape, jnp.int32),
+            pltpu.VMEM(tile_type.shape, jnp.int32),
             dma((chunks,)), dma((chunks,)), dma((chunks,)), dma((chunks,)), dma((chunks,)),
-            dma((chunks,)), dma((chunks,)), dma((2,)), dma((2,)), dma((2, chunks)),
+            dma((chunks,)), dma((chunks,)), dma((2,)), dma((2,)), dma((5,)),
         ],
         compiler_params=pltpu.CompilerParams(
-            collective_id=0, has_side_effects=True, vmem_limit_bytes=48 * 1024 * 1024),
+            collective_id=0, has_side_effects=True, vmem_limit_bytes=58 * 1024 * 1024 + 900 * 1024),
         cost_estimate=pl.CostEstimate(
             flops=2 * product_rows * depth * depth * blocks.shape[0], bytes_accessed=12 * all_rows * cells,
             transcendentals=0),
     )(flat, time_step, blocks, cut_counts, tile_index, tile_type)
+    pieces = 4
+    res, new = pl.pallas_call(
+        functools.partial(store, pieces),
+        out_shape=[jax.ShapeDtypeStruct(flat.shape, jnp.float32)] * 2,
+        in_specs=[anywhere, anywhere],
+        out_specs=[hbm, hbm],
+        scratch_shapes=[dma((2, pieces))],
+        compiler_params=pltpu.CompilerParams(vmem_limit_bytes=2 * 1024 * 1024),
+    )(res, new)
     return res.reshape(state.shape), new.reshape(state.shape)
 
 

time: 46.1 us -> 38.4 us (0.83)
  local copies, waits for them, and re-layouts: 8.62 us -> 0 us
  Pallas kernels: 36.5 us -> 37.6 us
    unnamed x14 -> x0, local copies, waits for them, and re-layouts: 8.62 us -> none
    pallas_call x1 -> x2, Pallas kernels: 36.5 us -> 37.6 us  [the longest x1 35.1 us: fused(): pl.pallas_call(functools.partial(kernel, sizes), out_shape=[pltpu.VMEM(fl...]
where the time goes in v2:
time: 38.4 us; the launch traced here: 38.2 us
  Pallas kernels  37.6 us (98%)
  between operations  0.64 us (2%)
    pallas_call x1, Pallas kernels, fused(): pl.pallas_call(functools.partial(kernel, sizes), out_shape=[pltpu.VMEM(fl...  35.1 us
    pallas_call x1, Pallas kernels, fused(): pl.pallas_call(functools.partial(store, pieces), out_shape=[jax.ShapeDtyp...  2.42 us

profile of v2, /device:TPU:0, one launch (start us, length us, event | category | flops | bytes accessed | tf_op | source)
XLA Modules:
  0.0 38.2 jit_solution(49836358914997795)
XLA Ops:
  0.6 35.1 %shard_map.77 = (f32[160,4096]{1,0:T(8,128)S(1)}, f32[160,4096]{1,0:T(8,128)S(1)}) custom-call(f32[160,4096]{1,0:T(8,128)} %bitcast.3, f32[8,4096]{1,0:T(8,128)} %step_in.1, bf16[8,320,320]{2,1,0:T(8,128)(2,1)} %blocks_in.1, s32[4]{0:T(128)} %counts_in.1, s32[1,256]{1,0:T(1,128)} %index_in.1, s32[1,256]{1,0:T(1,128)} %kinds_in.1), custom_call_target="tpu_custom_call" | custom-call | flops 6710886400 | bytes 7864320 | tf_op jit(solution)/shard_map/pallas_call | solution.py:308
  35.8 2.4 %shard_map.78 = (f32[160,4096]{1,0:T(8,128)}, f32[160,4096]{1,0:T(8,128)}) custom-call(f32[160,4096]{1,0:T(8,128)S(1)} %get-tuple-element.6.refs_0_, f32[160,4096]{1,0:T(8,128)S(1)} %get-tuple-element.7.refs_1_), custom_call_target="tpu_custom_call" | custom-call | tf_op jit(solution)/shard_map/pallas_call | solution.py:340

commit v3 on v2

--- a/solution.py
+++ b/solution.py
@@ -73,7 +73,21 @@
             halo_out.at[side], halo_in.at[side], halo_send.at[side], halo_recv.at[side],
             below if side == 0 else above, device_id_type=MESH)
 
-    @pl.loop(0, chunks)
+    fetch(0).start()
+
+    barrier = pltpu.get_barrier_semaphore()
+    pl.semaphore_signal(barrier, inc=1, device_id=sibling, device_id_type=MESH)
+    pl.semaphore_signal(barrier, inc=1, device_id=partner, device_id_type=MESH)
+
+    @pl.when(has_below)
+    def _():
+        pl.semaphore_signal(barrier, inc=1, device_id=below, device_id_type=MESH)
+
+    @pl.when(has_above)
+    def _():
+        pl.semaphore_signal(barrier, inc=1, device_id=above, device_id_type=MESH)
+
+    @pl.loop(1, chunks)
     def _(c):
         fetch(c).start()
 
@@ -85,28 +99,22 @@
     for copy in side:
         copy.start()
 
-    barrier = pltpu.get_barrier_semaphore()
-    pl.semaphore_signal(barrier, inc=1, device_id=sibling, device_id_type=MESH)
-    pl.semaphore_signal(barrier, inc=1, device_id=partner, device_id_type=MESH)
-
-    @pl.when(has_below)
-    def _():
-        pl.semaphore_signal(barrier, inc=1, device_id=below, device_id_type=MESH)
-
-    @pl.when(has_above)
-    def _():
-        pl.semaphore_signal(barrier, inc=1, device_id=above, device_id_type=MESH)
-
-    ends = n_brick - 1
-    pl.semaphore_wait(barrier, 2 + (brick + ends) // n_brick + (ends - brick + ends) // n_brick)
-
-    @pl.loop(0, chunks)
-    def _(c):
+    def round_part(c):
         fetch(c).wait()
         for v in range(nvar):
             block = jnp.concatenate(
                 [x[(i * nvar + v) * rows:(i * nvar + v + 1) * rows, lanes(c)] for i in range(inst)], axis=0)
             send[c, v * inst * rows:(v + 1) * inst * rows, :] = (block - CENTRE[v]).astype(jnp.bfloat16)
+
+    round_part(0)
+    ends = n_brick - 1
+    pl.semaphore_wait(barrier, 2 + (brick + ends) // n_brick + (ends - brick + ends) // n_brick)
+    to_partner(0).start()
+    to_sibling(0).start()
+
+    @pl.loop(1, chunks)
+    def _(c):
+        round_part(c)
         to_partner(c).start()
         to_sibling(c).start()
 
@@ -238,40 +246,50 @@
     d_cross = {m: spectral(m - half, total) for m in span}
     d_fwd = {m: choose(spectral(m - inst - half, total), spectral(m + inst - half, total)) for m in span}
 
-    def finish(c):
+    def near_part(c):
         at = lanes(c)
         for v in range(nvar):
-            cut = slice(v * inst * rows, (v + 1) * inst * rows)
-            one = cross[c, cut, :].astype(jnp.float32)
-            two = fwd[c, cut, :].astype(jnp.float32)
             for j in range(inst):
                 put = slice((j * nvar + v) * rows, (j * nvar + v + 1) * rows)
                 value = acc[put, at]
                 for k in range(inst):
                     take = slice((k * nvar + v) * rows, (k * nvar + v + 1) * rows)
-                    local = slice(k * rows, (k + 1) * rows)
-                    m = j - k
-                    if m:
-                        value = value + d_own[m] * (x[take, at] - CENTRE[v])
-                        value = value + d_cross[m] * one[local]
-                    value = value + d_sib[m] * (sib[take, at] - CENTRE[v])
-                    value = value + d_fwd[m] * two[local]
+                    if j != k:
+                        value = value + d_own[j - k] * (x[take, at] - CENTRE[v])
+                    value = value + d_sib[j - k] * (sib[take, at] - CENTRE[v])
                 acc[put, at] = value
-                fresh[put, at] = x[put, at] - step[:, at] * value
+
+    def far_part(c, source, table, last):
+        at = lanes(c)
+        for v in range(nvar):
+            block = source[c, v * inst * rows:(v + 1) * inst * rows, :].astype(jnp.float32)
+            for j in range(inst):
+                put = slice((j * nvar + v) * rows, (j * nvar + v + 1) * rows)
+                value = acc[put, at]
+                for k in range(inst):
+                    value = value + table[j - k] * block[k * rows:(k + 1) * rows]
+                acc[put, at] = value
+                if last:
+                    fresh[put, at] = x[put, at] - step[:, at] * value
 
     @pl.loop(0, chunks)
     def _(c):
         to_sibling(c).wait()
+        near_part(c)
+
+    @pl.loop(0, chunks)
+    def _(c):
         to_partner(c).wait()
         forward(c).start()
+        far_part(c, cross, d_cross, False)
 
         @pl.when(c > 0)
         def _():
             forward(c - 1).wait()
-            finish(c - 1)
+            far_part(c - 1, fwd, d_fwd, True)
 
     forward(chunks - 1).wait()
-    finish(chunks - 1)
+    far_part(chunks - 1, fwd, d_fwd, True)
 
 
 def store(chunks, *refs):

time: 38.4 us -> 38 us (0.990)
  Pallas kernels: 37.6 us -> 37.2 us
where the time goes in v3:
time: 38 us; the launch traced here: 37.9 us
  Pallas kernels  37.2 us (98%)
  between operations  0.64 us (2%)
    pallas_call x1, Pallas kernels, fused(): pl.pallas_call(functools.partial(kernel, sizes), out_shape=[pltpu.VMEM(fl...  34.8 us
    pallas_call x1, Pallas kernels, fused(): pl.pallas_call(functools.partial(store, pieces), out_shape=[jax.ShapeDtyp...  2.42 us

profile of v3, /device:TPU:0, one launch (start us, length us, event | category | flops | bytes accessed | tf_op | source)
XLA Modules:
  0.0 37.9 jit_solution(14848683868377302707)
XLA Ops:
  0.6 34.8 %shard_map.77 = (f32[160,4096]{1,0:T(8,128)S(1)}, f32[160,4096]{1,0:T(8,128)S(1)}) custom-call(f32[160,4096]{1,0:T(8,128)} %bitcast.3, f32[8,4096]{1,0:T(8,128)} %step_in.1, bf16[8,320,320]{2,1,0:T(8,128)(2,1)} %blocks_in.1, s32[4]{0:T(128)} %counts_in.1, s32[1,256]{1,0:T(1,128)} %index_in.1, s32[1,256]{1,0:T(1,128)} %kinds_in.1), custom_call_target="tpu_custom_call" | custom-call | flops 6710886400 | bytes 7864320 | tf_op jit(solution)/shard_map/pallas_call | solution.py:326
  35.4 2.4 %shard_map.78 = (f32[160,4096]{1,0:T(8,128)}, f32[160,4096]{1,0:T(8,128)}) custom-call(f32[160,4096]{1,0:T(8,128)S(1)} %get-tuple-element.6.refs_0_, f32[160,4096]{1,0:T(8,128)S(1)} %get-tuple-element.7.refs_1_), custom_call_target="tpu_custom_call" | custom-call | tf_op jit(solution)/shard_map/pallas_call | solution.py:358

commit v4 on v3

--- a/solution.py
+++ b/solution.py
@@ -312,7 +312,7 @@
     tile = blocks.shape[1] // nvar
     total = inst * mesh.shape["inst"]
     n_brick = mesh.shape["brick"]
-    chunks = 8
+    chunks = 4
     all_rows = inst * nvar * rows
     width = cells // chunks
     depth = nvar * LANES

time: 38 us -> 38.1 us (level)
  no operation moved by 1% of the time
where the time goes in v4:
time: 38.1 us; the launch traced here: 38 us
  Pallas kernels  37.3 us (98%)
  between operations  0.64 us (2%)
    pallas_call x1, Pallas kernels, fused(): pl.pallas_call(functools.partial(kernel, sizes), out_shape=[pltpu.VMEM(fl...  34.9 us
    pallas_call x1, Pallas kernels, fused(): pl.pallas_call(functools.partial(store, pieces), out_shape=[jax.ShapeDtyp...  2.42 us

profile of v4, /device:TPU:0, one launch (start us, length us, event | category | flops | bytes accessed | tf_op | source)
XLA Modules:
  0.0 38.0 jit_solution(22178154479242287)
XLA Ops:
  0.6 34.9 %shard_map.77 = (f32[160,4096]{1,0:T(8,128)S(1)}, f32[160,4096]{1,0:T(8,128)S(1)}) custom-call(f32[160,4096]{1,0:T(8,128)} %bitcast.3, f32[8,4096]{1,0:T(8,128)} %step_in.1, bf16[8,320,320]{2,1,0:T(8,128)(2,1)} %blocks_in.1, s32[4]{0:T(128)} %counts_in.1, s32[1,256]{1,0:T(1,128)} %index_in.1, s32[1,256]{1,0:T(1,128)} %kinds_in.1), custom_call_target="tpu_custom_call" | custom-call | flops 6710886400 | bytes 7864320 | tf_op jit(solution)/shard_map/pallas_call | solution.py:326
  35.6 2.4 %shard_map.78 = (f32[160,4096]{1,0:T(8,128)}, f32[160,4096]{1,0:T(8,128)}) custom-call(f32[160,4096]{1,0:T(8,128)S(1)} %get-tuple-element.6.refs_0_, f32[160,4096]{1,0:T(8,128)S(1)} %get-tuple-element.7.refs_1_), custom_call_target="tpu_custom_call" | custom-call | tf_op jit(solution)/shard_map/pallas_call | solution.py:358
